TPU v7x, 32 devices: a whole 2x2x4 slice. The times are simulated.
32 devices in a mesh: gx: 16 (over z, x, core), gz: 2 (over y).
Axes of the slice: x: 2, y: 2, z: 4, core: 2. Of those that a mesh axis runs over, the one named last changes fastest.
Arguments:
- right_side: float32 [3, 6, 128, 1024], P(None, 'gz', 'gx'), may hold values from -48 to 48
- density: float32 [6, 128, 1024], P('gz', 'gx'), may hold values from 0.5 to 4
Outputs:
- solution_field: float32 [3, 6, 128, 1024], P(None, 'gz', 'gx')
All inputs are finite; a program needn't handle non-finite values.
Results may differ from a plain program's by a relative error of at most 0.0001.
Values sent between devices are 32-bit elements; how exact they have to be, the bound alone decides.
A program may use at most 128 MiB of HBM per device.

v0:
```python
import functools
import jax
import jax.numpy as jnp
from jax import lax
from jax.experimental import pallas as pl
from jax.experimental.pallas import tpu as pltpu
from jax.sharding import PartitionSpec as P

LEVELS = 4
CYCLES = 2
relaxation = 0.8
plane_coupling = 16.0
depth_coupling = 1.0
SUB, LANE = 8, 128
COUPLING = [plane_coupling / 4.0**level for level in range(LEVELS)]
HALO = [5, 2, 2, 2]
MESH = pl.DeviceIdType.MESH


def iotas():
    return (
        lax.broadcasted_iota(jnp.int32, (SUB, LANE), 0),
        lax.broadcasted_iota(jnp.int32, (SUB, LANE), 1),
    )


def y_sum(v, k):
    sub, lane = iotas()
    from_low = pltpu.roll(v, k, 2)
    from_high = pltpu.roll(v, LANE - k, 2)
    low_carry = jnp.where(sub == 0, 0.0, pltpu.roll(from_low, 1, 1))
    high_carry = jnp.where(sub == SUB - 1, 0.0, pltpu.roll(from_high, SUB - 1, 1))
    return jnp.where(lane < k, low_carry, from_low) + jnp.where(lane >= LANE - k, high_carry, from_high)


def neighbours(src, row, c, v, level):
    lateral = src[row - 1, c] + src[row + 1, c] + y_sum(v, 1 << level)
    vertical = jnp.concatenate([v[-1:], v[:-1]], 0) + jnp.concatenate([v[1:], v[:1]], 0)
    return COUPLING[level] * lateral + depth_coupling * vertical


def pair_sum(v, level):
    k = 1 << level
    _, lane = iotas()
    low = (lane & k) == 0
    return v + jnp.where(low, pltpu.roll(v, LANE - k, 2), pltpu.roll(v, k, 2))


def pack(planes, p):
    if p == 1:
        return planes
    _, lane = iotas()
    groups = -(-len(planes) // p)
    out = []
    for g in range(groups):
        value = planes[g]
        for j in range(1, p):
            if j * groups + g < len(planes):
                value = jnp.where((lane & (p - 1)) == j, planes[j * groups + g], value)
        out.append(value)
    return out


def unpack(groups, count, p):
    _, lane = iotas()
    out = []
    for index in range(count):
        j, g = divmod(index, len(groups))
        value, bit = groups[g], 1
        while bit < p:
            if j & bit:
                value = jnp.where((lane & bit) != 0, value, pltpu.roll(value, LANE - bit, 1))
            else:
                value = jnp.where((lane & bit) == 0, value, pltpu.roll(value, bit, 1))
            bit *= 2
        out.append(value)
    return out


def kernel(plan, block, out, *scratch):
    nx_dev, nz_dev, comps, nz_own, nz, rows = (
        plan[k] for k in ("gx", "gz", "comps", "nz_own", "nz", "rows"))
    refs = dict(zip(plan["names"], scratch))
    send_sem, recv_sem, local_sem = refs["send"], refs["recv"], refs["local"]
    me, mz = lax.axis_index("gx"), lax.axis_index("gz")
    z0 = mz * nz_own
    counter = [0]

    def there(offset):
        target = me + offset
        return jnp.logical_and(target >= 0, target < nx_dev)

    offsets = (-1, 1, -2, 2)
    barrier = pltpu.get_barrier_semaphore()
    expected = nz_dev - 1
    for step in range(1, nz_dev):
        pl.semaphore_signal(barrier, inc=1, device_id={"gz": lax.rem(mz + step, nz_dev)}, device_id_type=MESH)
    for offset in offsets:
        expected = expected + there(offset).astype(jnp.int32)

        @pl.when(there(offset))
        def _():
            pl.semaphore_signal(barrier, inc=1, device_id={"gx": me + offset}, device_id_type=MESH)

    pl.semaphore_wait(barrier, expected)

    def send(offset, src, dst):
        index = counter[0]
        counter[0] += 1
        copy = pltpu.make_async_remote_copy(
            src_ref=src, dst_ref=dst, send_sem=send_sem.at[index], recv_sem=recv_sem.at[index],
            device_id={"gx": me + offset}, device_id_type=MESH)

        @pl.when(there(offset))
        def _():
            copy.start()

        def finish(received=lambda: None, absent=lambda: None):
            @pl.when(there(offset))
            def _():
                copy.wait_send()

            @pl.when(there(-offset))
            def _():
                copy.wait_recv()
                received()

            @pl.when(jnp.logical_not(there(-offset)))
            def _():
                absent()

        return finish

    def zero_rows(ref, low, high):
        def run():
            for row in range(low, high):
                ref[row] = jnp.zeros(ref.shape[1:], ref.dtype)
        return run

    s0 = refs["s0"]
    h0 = HALO[0]
    own = s0.at[pl.ds(h0, rows[0]), :, pl.ds(z0, nz_own)]
    local = pltpu.make_async_copy(block, own, local_sem)
    local.start()
    gathers = []
    for step in range(1, nz_dev):
        index = counter[0]
        counter[0] += 1
        copy = pltpu.make_async_remote_copy(
            src_ref=block, dst_ref=own, send_sem=send_sem.at[index], recv_sem=recv_sem.at[index],
            device_id={"gz": lax.rem(mz + step, nz_dev)}, device_id_type=MESH)
        copy.start()
        gathers.append(copy)
    local.wait()
    for copy in gathers:
        copy.wait()

    n0 = rows[0]
    near = [
        send(-1, s0.at[h0:h0 + 2], s0.at[h0 + n0:h0 + n0 + 2]),
        send(1, s0.at[h0 + n0 - 2:h0 + n0], s0.at[h0 - 2:h0]),
    ]
    far = [
        send(-1, s0.at[h0 + 2:h0 + 4], s0.at[h0 + n0 + 2:h0 + n0 + 4]),
        send(1, s0.at[h0 + n0 - 4:h0 + n0 - 2], s0.at[h0 - 4:h0 - 2]),
    ]

    def loop(low, high, body):
        lax.fori_loop(low, high, lambda row, carry: (body(row), 0)[1], 0)

    def weights(level, low, high):
        s, w, h, n = refs[f"s{level}"], refs[f"w{level}"], HALO[level], rows[level]

        def body(row):
            place = row - h + me * n
            inside = jnp.logical_and(place >= 0, place < n * nx_dev)
            scale = jnp.where(inside, relaxation, 0.0).astype(jnp.float32)
            w[row] = scale / (s[row, comps] + 4.0 * COUPLING[level] + 2.0 * depth_coupling)

        loop(h + low, h + high, body)

    def first_sweep(level, dst, extra):
        s, w, h, n = refs[f"s{level}"], refs[f"w{level}"], HALO[level], rows[level]

        def body(row):
            weight = w[row]
            for c in range(comps):
                dst[row, c] = weight * s[row, c]

        loop(h - extra, h + n + extra, body)

    def sweep(level, src, dst, extra, last=False):
        s, w, h, n = refs[f"s{level}"], refs[f"w{level}"], HALO[level], rows[level]

        def body(row):
            weight = w[row]
            for c in range(comps):
                v = src[row, c]
                dst[row, c] = (1.0 - relaxation) * v + weight * (s[row, c] + neighbours(src, row, c, v, level))
            if last:
                out[row - h] = dst[row, :, pl.ds(z0, nz_own)]

        loop(h - extra, h + n + extra, body)

    def restrict(level, src, with_density):
        s, h, n = refs[f"s{level}"], HALO[level], rows[level]
        coarse, hc = refs[f"s{level + 1}"], HALO[level + 1]

        def body(index):
            for c in range(comps):
                total = None
                for part in range(2):
                    row = h + 2 * index + part
                    v = src[row, c]
                    diagonal = s[row, comps] + 4.0 * COUPLING[level] + 2.0 * depth_coupling
                    value = s[row, c] - diagonal * v + neighbours(src, row, c, v, level)
                    total = value if total is None else total + value
                coarse[hc + index, c] = 0.25 * pair_sum(total, level)
            if with_density:
                total = s[h + 2 * index, comps] + s[h + 2 * index + 1, comps]
                coarse[hc + index, comps] = 0.25 * pair_sum(total, level)

        loop(0, rows[level + 1], body)

    def halo(level, ref, count, tag):
        p, h, n = 1 << level, HALO[level], rows[level]
        out_buf, in_buf = refs[f"out_{tag}"], refs[f"in_{tag}"]
        for row in range(n):
            planes = [ref[h + row, c, z] for c in range(count) for z in range(nz)]
            for g, value in enumerate(pack(planes, p)):
                out_buf[row, g] = value
        finishes = []
        width = min(n, 2)
        for slot, offset in enumerate(offsets if n == 1 else offsets[:2]):
            first = 0 if offset < 0 else n - width
            finishes.append((send(offset, out_buf.at[first:first + width], in_buf.at[slot]), slot, offset))
        for finish, slot, offset in finishes:
            if n == 1:
                start = h - offset
            else:
                start = h + n if offset < 0 else h - width

            def received(slot=slot, start=start):
                for row in range(width):
                    groups = [in_buf[slot, row, g] for g in range(in_buf.shape[2])]
                    for index, value in enumerate(unpack(groups, count * nz, p)):
                        ref[start + row, index // nz, index % nz] = value

            finish(received, zero_rows(ref, start, start + width))

    def correct(level, field, dst):
        h, n = HALO[level], rows[level]
        hc = HALO[level + 1]
        coarse = refs[f"a{level + 1}"]

        def body(index):
            for part in range(2):
                for c in range(comps):
                    dst[h + 2 * index + part, c] = field[h + 2 * index + part, c] + coarse[hc + index, c]

        loop(0, rows[level + 1], body)

    def coarse_cycle(level, cycle):
        s, a, b = refs[f"s{level}"], refs[f"a{level}"], refs[f"b{level}"]
        h, n = HALO[level], rows[level]
        halo(level, s, comps + (1 if cycle == 0 else 0), f"s{level}_{cycle}")
        if cycle == 0:
            weights(level, -2, n + 2)
        first_sweep(level, a, 2)
        sweep(level, a, b, 1)
        if level == LEVELS - 1:
            sweep(level, b, a, 0)
            return
        restrict(level, b, cycle == 0)
        coarse_cycle(level + 1, cycle)
        correct(level, b, a)
        halo(level, a, comps, f"v{level}_{cycle}")
        sweep(level, a, b, 1)
        sweep(level, b, a, 0)

    a0, b0 = refs["a0"], refs["b0"]
    near[0](absent=zero_rows(s0, h0 + n0, h0 + n0 + 2))
    near[1](absent=zero_rows(s0, h0 - 2, h0))
    weights(0, -2, n0 + 2)
    first_sweep(0, a0, 2)
    for cycle in range(CYCLES):
        if cycle == 0:
            sweep(0, a0, b0, 1)
        restrict(0, b0, cycle == 0)
        coarse_cycle(1, cycle)
        fresh = refs[f"f{cycle}"]
        correct(0, b0, fresh)
        wide = 5 if cycle < CYCLES - 1 else 2
        ends = [
            send(-1, fresh.at[h0:h0 + wide], fresh.at[h0 + n0:h0 + n0 + wide]),
            send(1, fresh.at[h0 + n0 - wide:h0 + n0], fresh.at[h0 - wide:h0]),
        ]
        if cycle == 0:
            far[0](absent=zero_rows(s0, h0 + n0 + 2, h0 + n0 + 4))
            far[1](absent=zero_rows(s0, h0 - 4, h0 - 2))
            weights(0, -4, -2)
            weights(0, n0 + 2, n0 + 4)
        ends[0](absent=zero_rows(fresh, h0 + n0, h0 + n0 + wide))
        ends[1](absent=zero_rows(fresh, h0 - wide, h0))
        if cycle < CYCLES - 1:
            sweep(0, fresh, a0, 4)
            sweep(0, a0, b0, 3)
            sweep(0, b0, a0, 2)
            sweep(0, a0, b0, 1)
        else:
            sweep(0, fresh, a0, 1)
            sweep(0, a0, b0, 0, last=True)


def shards(plan, right_side, density):
    comps, nz_own, n0, ny = right_side.shape
    block = jnp.concatenate([right_side, density[None]], 0)
    block = block.reshape(comps + 1, nz_own, n0, SUB, LANE).transpose(2, 0, 1, 3, 4)
    nz = nz_own * plan["gz"]
    rows = [n0 >> level for level in range(LEVELS)]
    shapes = {}

    def buf(name, *shape):
        shapes[name] = pltpu.VMEM(shape + (SUB, LANE), jnp.float32)

    for level in range(LEVELS):
        total = rows[level] + 2 * HALO[level]
        buf(f"s{level}", total, comps + 1, nz)
        buf(f"w{level}", total, nz)
        buf(f"a{level}", total, comps, nz)
        buf(f"b{level}", total, comps, nz)
    for cycle in range(CYCLES):
        buf(f"f{cycle}", rows[0] + 2 * HALO[0], comps, nz)
        for level in range(1, LEVELS):
            n = rows[level]
            for kind, count in (("s", comps + (cycle == 0)), ("v", comps)):
                if kind == "v" and level == LEVELS - 1:
                    continue
                groups = -(-count * nz // (1 << level))
                buf(f"out_{kind}{level}_{cycle}", n, groups)
                buf(f"in_{kind}{level}_{cycle}", 4 if n == 1 else 2, min(n, 2), groups)
    sems = plan["gz"] - 1 + 4 + CYCLES * (2 + 2 * 2 * (LEVELS - 2) + 4)
    shapes["send"] = pltpu.SemaphoreType.DMA((sems,))
    shapes["recv"] = pltpu.SemaphoreType.DMA((sems,))
    shapes["local"] = pltpu.SemaphoreType.DMA
    plan = dict(plan, comps=comps, nz_own=nz_own, nz=nz, rows=rows, names=list(shapes))
    result = pl.pallas_call(
        functools.partial(kernel, plan),
        out_shape=jax.ShapeDtypeStruct((n0, comps, nz_own, SUB, LANE), jnp.float32),
        in_specs=[pl.BlockSpec(memory_space=pltpu.VMEM)],
        out_specs=pl.BlockSpec(memory_space=pltpu.VMEM),
        scratch_shapes=list(shapes.values()),
        compiler_params=pltpu.CompilerParams(
            collective_id=0, has_side_effects=True, vmem_limit_bytes=60 * 1024 * 1024),
    )(block)
    return result.transpose(1, 2, 0, 3, 4).reshape(comps, nz_own, n0, ny)


def solution(mesh):
    plan = dict(gx=mesh.shape["gx"], gz=mesh.shape["gz"])
    return jax.shard_map(
        functools.partial(shards, plan),
        mesh=mesh,
        in_specs=(P(None, "gz", "gx", None), P("gz", "gx", None)),
        out_specs=P(None, "gz", "gx", None),
        check_vma=False,
    )
```

profile of v0, /device:TPU:3, one launch (start us, length us, event | category | flops | bytes accessed | tf_op | source)
XLA Modules:
  0.0 94.8 jit_solution(13959400309999116581)
XLA Ops:
  0.0 0.9 copy.14
  0.9 1.0 %copy.10 = f32[9,8,8,128]{3,2,1,0:T(8,128)S(1)} copy(f32[9,8,8,128]{3,1,2,0:T(8,128)} %bitcast.19) | data formatting | bytes 589824
  1.9 0.8 copy_bitcast_fusion.block
  2.7 90.3 %shard_map.28 = f32[8,3,3,8,128]{4,3,2,1,0:T(8,128)} custom-call(f32[8,4,3,8,128]{4,3,2,1,0:T(8,128)} %copy_bitcast_fusion.block), custom_call_target="tpu_custom_call" | custom-call | tf_op jit(solution)/shard_map/pallas_call | solution.py:347
  93.0 1.0 %copy.8 = f32[3,3,8,8,128]{4,3,2,1,0:T(8,128)S(1)} copy(f32[3,3,8,8,128]{4,3,1,0,2:T(8,128)} %bitcast.17) | data formatting | bytes 589824 | tf_op jit(solution)/shard_map/transpose | solution.py:356
  94.0 0.8 reshape.7
where the time goes:
time: 95.5 us; the launch traced here: 94.8 us
  Pallas kernels  90.3 us (95%)
  local copies, waits for them, and re-layouts  3.68 us (4%)
    pallas_call x1, Pallas kernels, shards(): pl.pallas_call(functools.partial(kernel, plan), out_shape=jax.ShapeDtypeS...  90.3 us
    unnamed x2, local copies, waits for them, and re-layouts  1.93 us

commit v1 on v0

v1 whole, which is shorter than its diff:
```python
import functools
import jax
import jax.numpy as jnp
from jax import lax
from jax.experimental import pallas as pl
from jax.experimental.pallas import tpu as pltpu
from jax.sharding import PartitionSpec as P

LEVELS = 4
CYCLES = 2
relaxation = 0.8
plane_coupling = 16.0
depth_coupling = 1.0
SUB, LANE = 8, 128
COUPLING = [plane_coupling / 4.0**level for level in range(LEVELS)]
HALO = [5, 2, 2, 2]
SKEW = 0
MESH = pl.DeviceIdType.MESH


def iotas():
    return (
        lax.broadcasted_iota(jnp.int32, (SUB, LANE), 0),
        lax.broadcasted_iota(jnp.int32, (SUB, LANE), 1),
    )


def y_sum(v, k):
    shape = v.shape
    v = v.reshape((-1, SUB, LANE))
    sub, lane = iotas()
    from_low = pltpu.roll(v, k, 2)
    from_high = pltpu.roll(v, LANE - k, 2)
    low_carry = jnp.where(sub == 0, 0.0, pltpu.roll(from_low, 1, 1))
    high_carry = jnp.where(sub == SUB - 1, 0.0, pltpu.roll(from_high, SUB - 1, 1))
    total = jnp.where(lane < k, low_carry, from_low) + jnp.where(lane >= LANE - k, high_carry, from_high)
    return total.reshape(shape)


def neighbours(strip, level):
    v = strip[1:-1]
    lateral = strip[:-2] + strip[2:] + y_sum(v, 1 << level)
    vertical = jnp.concatenate([v[:, -1:], v[:, :-1]], 1) + jnp.concatenate([v[:, 1:], v[:, :1]], 1)
    return COUPLING[level] * lateral + depth_coupling * vertical


def pair_sum(v, level):
    k = 1 << level
    _, lane = iotas()
    low = (lane & k) == 0
    return v + jnp.where(low, pltpu.roll(v, LANE - k, 2), pltpu.roll(v, k, 2))


def pack(planes, p):
    if p == 1:
        return planes
    _, lane = iotas()
    groups = -(-len(planes) // p)
    out = []
    for g in range(groups):
        value = planes[g]
        for j in range(1, p):
            if j * groups + g < len(planes):
                value = jnp.where((lane & (p - 1)) == j, planes[j * groups + g], value)
        out.append(value)
    return out


def unpack(groups, count, p):
    _, lane = iotas()
    out = []
    for index in range(count):
        j, g = divmod(index, len(groups))
        value, bit = groups[g], 1
        while bit < p:
            if j & bit:
                value = jnp.where((lane & bit) != 0, value, pltpu.roll(value, LANE - bit, 1))
            else:
                value = jnp.where((lane & bit) == 0, value, pltpu.roll(value, bit, 1))
            bit *= 2
        out.append(value)
    return out


def kernel(plan, block, out, *scratch):
    nx_dev, nz_dev, comps, nz_own, nz, rows = (
        plan[k] for k in ("gx", "gz", "comps", "nz_own", "nz", "rows"))
    refs = dict(zip(plan["names"], scratch))
    send_sem, recv_sem, local_sem = refs["send"], refs["recv"], refs["local"]
    me, mz = lax.axis_index("gx"), lax.axis_index("gz")
    z0 = mz * nz_own
    counter = [0]
    dens = comps

    def there(offset):
        target = me + offset
        return jnp.logical_and(target >= 0, target < nx_dev)

    offsets = (-1, 1, -2, 2)
    barrier = pltpu.get_barrier_semaphore()
    expected = nz_dev - 1
    for step in range(1, nz_dev):
        pl.semaphore_signal(barrier, inc=1, device_id={"gz": lax.rem(mz + step, nz_dev)}, device_id_type=MESH)
    for offset in offsets:
        expected = expected + there(offset).astype(jnp.int32)

        @pl.when(there(offset))
        def _():
            pl.semaphore_signal(barrier, inc=1, device_id={"gx": me + offset}, device_id_type=MESH)

    pl.semaphore_wait(barrier, expected)

    def send(offset, src, dst):
        index = counter[0]
        counter[0] += 1
        copy = pltpu.make_async_remote_copy(
            src_ref=src, dst_ref=dst, send_sem=send_sem.at[index], recv_sem=recv_sem.at[index],
            device_id={"gx": me + offset}, device_id_type=MESH)

        @pl.when(there(offset))
        def _():
            copy.start()

        def finish(received=lambda: None, absent=lambda: None):
            @pl.when(there(-offset))
            def _():
                copy.wait_recv()
                received()

            @pl.when(jnp.logical_not(there(-offset)))
            def _():
                absent()

            @pl.when(there(offset))
            def _():
                copy.wait_send()

        return finish

    def zero_rows(ref, low, high):
        def run():
            for row in range(low, high):
                ref[row] = jnp.zeros(ref.shape[1:], ref.dtype)
        return run

    def loop(low, high, body):
        step = 2 if (high - low) % 2 == 0 else 1
        count = (high - low) // step
        if count <= 2 or step == 1:
            for index in range(count):
                body(low + index * step, step)
        else:
            lax.fori_loop(0, count, lambda i, carry: (body(low + i * step, step), 0)[1], 0)

    def weights(level, low, high):
        s, w, h, n = refs[f"s{level}"].at[dens], refs[f"w{level}"], HALO[level], rows[level]
        for row in range(h + low, h + high):
            place = row - h + me * n
            inside = jnp.logical_and(place >= 0, place < n * nx_dev)
            scale = jnp.where(inside, relaxation, 0.0).astype(jnp.float32)
            w[row] = scale / (s[row] + 4.0 * COUPLING[level] + 2.0 * depth_coupling)

    def first_sweep(level, c, dst, extra):
        s, w, h, n = refs[f"s{level}"].at[c], refs[f"w{level}"], HALO[level], rows[level]

        def body(row, m):
            here = pl.ds(row, m)
            dst[here] = w[here] * s[here]

        loop(h - extra, h + n + extra, body)

    def sweep(level, c, src, dst, extra, last=False):
        s, w, h, n = refs[f"s{level}"].at[c], refs[f"w{level}"], HALO[level], rows[level]

        def body(row, m):
            here = pl.ds(row, m)
            strip = src[pl.ds(row - 1, m + 2)]
            dst[here] = (1.0 - relaxation) * strip[1:-1] + w[here] * (s[here] + neighbours(strip, level))
            if last:
                out[c, pl.ds(row - h, m)] = dst[here, pl.ds(z0, nz_own)]

        loop(h - extra, h + n + extra, body)

    def restrict(level, c, src):
        s, d, h = refs[f"s{level}"].at[c], refs[f"s{level}"].at[dens], HALO[level]
        coarse, hc = refs[f"s{level + 1}"].at[c], HALO[level + 1]

        def body(row, m):
            here = pl.ds(row, m)
            strip = src[pl.ds(row - 1, m + 2)]
            diagonal = d[here] + 4.0 * COUPLING[level] + 2.0 * depth_coupling
            value = s[here] - diagonal * strip[1:-1] + neighbours(strip, level)
            place = hc + (row - h) // 2
            coarse[place] = 0.25 * pair_sum(value[0] + value[1], level)

        loop(h, h + rows[level], body)

    def restrict_density(level):
        fine, h = refs[f"s{level}"].at[dens], HALO[level]
        coarse, hc = refs[f"s{level + 1}"].at[dens], HALO[level + 1]
        for index in range(rows[level + 1]):
            coarse[hc + index] = 0.25 * pair_sum(fine[h + 2 * index] + fine[h + 2 * index + 1], level)

    def halo(level, ref, tag, c):
        p, h, n = 1 << level, HALO[level], rows[level]
        out_buf, in_buf = refs[f"out_{tag}"].at[c], refs[f"in_{tag}"].at[c]
        for row in range(n):
            for g, value in enumerate(pack([ref[h + row, z] for z in range(nz)], p)):
                out_buf[row, g] = value
        finishes = []
        width = min(n, 2)
        for slot, offset in enumerate(offsets if n == 1 else offsets[:2]):
            first = 0 if offset < 0 else n - width
            finishes.append((send(offset, out_buf.at[first:first + width], in_buf.at[slot]), slot, offset))

        def finish_all():
            for finish, slot, offset in finishes:
                if n == 1:
                    start = h - offset
                else:
                    start = h + n if offset < 0 else h - width

                def received(slot=slot, start=start):
                    for row in range(width):
                        groups = [in_buf[slot, row, g] for g in range(in_buf.shape[2])]
                        for z, value in enumerate(unpack(groups, nz, p)):
                            ref[start + row, z] = value

                finish(received, zero_rows(ref, start, start + width))

        return finish_all

    def correct(level, c, field, dst):
        h, n, hc = HALO[level], rows[level], HALO[level + 1]
        coarse = refs[f"a{level + 1}"].at[c]
        for index in range(rows[level + 1]):
            value = coarse[hc + index]
            for part in range(2):
                row = h + 2 * index + part
                dst[row] = field[row] + value

    h0, n0 = HALO[0], rows[0]
    s0 = refs["s0"]

    def gather(c):
        own = s0.at[c, pl.ds(h0, n0), pl.ds(z0, nz_own)]
        copies = [pltpu.make_async_copy(block.at[c], own, local_sem.at[c])]
        for step in range(1, nz_dev):
            index = counter[0]
            counter[0] += 1
            copies.append(pltpu.make_async_remote_copy(
                src_ref=block.at[c], dst_ref=own, send_sem=send_sem.at[index], recv_sem=recv_sem.at[index],
                device_id={"gz": lax.rem(mz + step, nz_dev)}, device_id_type=MESH))
        for copy in reversed(copies):
            copy.start()

        def finish():
            for copy in copies:
                copy.wait()

        return finish

    def ends(ref, skip, width):
        low, high = h0 + n0 + skip, h0 - skip
        left = send(-1, ref.at[h0 + skip:h0 + skip + width], ref.at[low:low + width])
        right = send(1, ref.at[h0 + n0 - skip - width:h0 + n0 - skip], ref.at[high - width:high])

        def finish():
            left(absent=zero_rows(ref, low, low + width))
            right(absent=zero_rows(ref, high - width, high))

        return finish

    density = {}

    def coarse_cycle(level, c, cycle):
        s, a, b = (refs[f"{kind}{level}"].at[c] for kind in "sab")
        h, n = HALO[level], rows[level]
        finish = halo(level, s, f"s{level}_{cycle}", c)
        yield
        if cycle == 0 and c == 0:
            density.pop(level)()
            weights(level, -2, n + 2)
        finish()
        first_sweep(level, c, a, 2)
        sweep(level, c, a, b, 1)
        if level == LEVELS - 1:
            sweep(level, c, b, a, 0)
            return
        restrict(level, c, b)
        yield from coarse_cycle(level + 1, c, cycle)
        correct(level, c, b, a)
        finish = halo(level, a, f"v{level}_{cycle}", c)
        yield
        finish()
        sweep(level, c, a, b, 1)
        sweep(level, c, b, a, 0)

    gathers = {c: gather(c) for c in [dens] + list(range(comps))}

    def component(c):
        a0, b0 = refs["a0"].at[c], refs["b0"].at[c]
        if c == 0:
            gathers[dens]()
            density["near"] = ends(s0.at[dens], 0, 2)
        gathers[c]()
        finish = ends(s0.at[c], 0, 2)
        if c == 0:
            for level in range(LEVELS - 1):
                restrict_density(level)
        yield
        if c == 0:
            density.pop("near")()
            weights(0, -2, n0 + 2)
            for level in range(1, LEVELS):
                density[level] = halo(level, refs[f"s{level}"].at[dens], f"s{level}_0", dens)
            density["far"] = ends(s0.at[dens], 2, 2)
        finish()
        far = ends(s0.at[c], 2, 2)
        first_sweep(0, c, a0, 2)
        sweep(0, c, a0, b0, 1)
        for cycle in range(CYCLES):
            restrict(0, c, b0)
            yield from coarse_cycle(1, c, cycle)
            fresh = refs[f"f{cycle}"].at[c]
            correct(0, c, b0, fresh)
            finish = ends(fresh, 0, 5 if cycle < CYCLES - 1 else 2)
            yield
            if cycle == 0:
                if c == 0:
                    density.pop("far")()
                    weights(0, -4, -2)
                    weights(0, n0 + 2, n0 + 4)
                far()
            finish()
            if cycle < CYCLES - 1:
                sweep(0, c, fresh, a0, 4)
                sweep(0, c, a0, b0, 3)
                sweep(0, c, b0, a0, 2)
                sweep(0, c, a0, b0, 1)
            else:
                sweep(0, c, fresh, a0, 1)
                sweep(0, c, a0, b0, 0, last=True)

    waiting = [component(c) for c in range(comps)]
    turn = 0
    while any(part is not None for part in waiting):
        for c in range(comps):
            if waiting[c] is not None and turn >= c * SKEW:
                try:
                    next(waiting[c])
                except StopIteration:
                    waiting[c] = None
        turn += 1
    assert counter[0] == send_sem.shape[0]


def shards(plan, right_side, density):
    comps, nz_own, n0, ny = right_side.shape
    block = jnp.concatenate([right_side, density[None]], 0)
    block = block.reshape(comps + 1, nz_own, n0, SUB, LANE).transpose(0, 2, 1, 3, 4)
    nz = nz_own * plan["gz"]
    rows = [n0 >> level for level in range(LEVELS)]
    shapes = {}

    def buf(name, *shape):
        shapes[name] = pltpu.VMEM(shape + (SUB, LANE), jnp.float32)

    for level in range(LEVELS):
        total = rows[level] + 2 * HALO[level]
        buf(f"s{level}", comps + 1, total, nz)
        buf(f"w{level}", total, nz)
        buf(f"a{level}", comps, total, nz)
        buf(f"b{level}", comps, total, nz)
    sems = (comps + 1) * (plan["gz"] - 1)
    for cycle in range(CYCLES):
        buf(f"f{cycle}", comps, rows[0] + 2 * HALO[0], nz)
        sems += comps * 2
        for level in range(1, LEVELS):
            n = rows[level]
            for kind, count in (("s", comps + (cycle == 0)), ("v", comps)):
                if kind == "v" and level == LEVELS - 1:
                    continue
                groups = -(-nz // (1 << level))
                buf(f"out_{kind}{level}_{cycle}", count, n, groups)
                buf(f"in_{kind}{level}_{cycle}", count, 4 if n == 1 else 2, min(n, 2), groups)
                sems += count * (4 if n == 1 else 2)
    sems += (comps + 1) * 4
    shapes["send"] = pltpu.SemaphoreType.DMA((sems,))
    shapes["recv"] = pltpu.SemaphoreType.DMA((sems,))
    shapes["local"] = pltpu.SemaphoreType.DMA((comps + 1,))
    plan = dict(plan, comps=comps, nz_own=nz_own, nz=nz, rows=rows, names=list(shapes))
    result = pl.pallas_call(
        functools.partial(kernel, plan),
        out_shape=jax.ShapeDtypeStruct((comps, n0, nz_own, SUB, LANE), jnp.float32),
        in_specs=[pl.BlockSpec(memory_space=pltpu.VMEM)],
        out_specs=pl.BlockSpec(memory_space=pltpu.VMEM),
        scratch_shapes=list(shapes.values()),
        compiler_params=pltpu.CompilerParams(
            collective_id=0, has_side_effects=True, vmem_limit_bytes=60 * 1024 * 1024),
    )(block)
    return result.transpose(0, 2, 1, 3, 4).reshape(comps, nz_own, n0, ny)


def solution(mesh):
    plan = dict(gx=mesh.shape["gx"], gz=mesh.shape["gz"])
    return jax.shard_map(
        functools.partial(shards, plan),
        mesh=mesh,
        in_specs=(P(None, "gz", "gx", None), P("gz", "gx", None)),
        out_specs=P(None, "gz", "gx", None),
        check_vma=False,
    )
```

time: 95.5 us -> 80.6 us (0.84)
  Pallas kernels: 90.3 us -> 75.9 us
    pallas_call x1, Pallas kernels: 90.3 us -> 75.9 us  [shards(): pl.pallas_call(functools.partial(kernel, plan), out_shape=jax.ShapeDtypeS...]
where the time goes in v1:
time: 80.6 us; the launch traced here: 80.4 us
  Pallas kernels  75.9 us (94%)
  local copies, waits for them, and re-layouts  3.68 us (5%)
    pallas_call x1, Pallas kernels, shards(): pl.pallas_call(functools.partial(kernel, plan), out_shape=jax.ShapeDtypeS...  75.9 us
    unnamed x2, local copies, waits for them, and re-layouts  1.93 us

profile of v1, /device:TPU:3, one launch (start us, length us, event | category | flops | bytes accessed | tf_op | source)
XLA Modules:
  0.0 80.4 jit_solution(3757042730429239603)
XLA Ops:
  0.0 0.9 %copy.14 = f32[3,8,8,128]{3,2,1,0:T(8,128)S(1)} copy(f32[3,8,8,128]{3,1,2,0:T(8,128)} %bitcast.20) | data formatting | bytes 196608
  0.9 1.0 %copy.10 = f32[9,8,8,128]{3,2,1,0:T(8,128)S(1)} copy(f32[9,8,8,128]{3,1,2,0:T(8,128)} %bitcast.19) | data formatting | bytes 589824
  1.9 0.8 copy_bitcast_fusion.block
  2.7 75.9 %shard_map.28 = f32[3,8,3,8,128]{4,3,2,1,0:T(8,128)} custom-call(f32[4,8,3,8,128]{4,3,2,1,0:T(8,128)} %copy_bitcast_fusion.block), custom_call_target="tpu_custom_call" | custom-call | tf_op jit(solution)/shard_map/pallas_call | solution.py:393
  78.6 1.0 %copy.8 = f32[3,3,8,8,128]{4,3,2,1,0:T(8,128)S(1)} copy(f32[3,3,8,8,128]{4,3,1,2,0:T(8,128)} %bitcast.17) | data formatting | bytes 589824 | tf_op jit(solution)/shard_map/transpose | solution.py:402
  79.6 0.8 reshape.7

commit v2 on v1

--- a/solution.py
+++ b/solution.py
@@ -13,7 +13,13 @@
 depth_coupling = 1.0
 SUB, LANE = 8, 128
 COUPLING = [plane_coupling / 4.0**level for level in range(LEVELS)]
-HALO = [5, 2, 2, 2]
+MERGED = False
+BEYOND = [[5, 3, 3, 3] if MERGED else [0, 0, 1, 2], [0, 0, 1, 2]]
+REACH = [
+    [6 if MERGED else 2] + [BEYOND[cycle][level] + (3 if level < LEVELS - 1 else 2) for level in range(1, LEVELS)]
+    for cycle in range(CYCLES)
+]
+HALO = [6 if MERGED else 5] + REACH[0][1:]
 SKEW = 0
 MESH = pl.DeviceIdType.MESH
 
@@ -41,7 +47,7 @@
     v = strip[1:-1]
     lateral = strip[:-2] + strip[2:] + y_sum(v, 1 << level)
     vertical = jnp.concatenate([v[:, -1:], v[:, :-1]], 1) + jnp.concatenate([v[:, 1:], v[:, :1]], 1)
-    return COUPLING[level] * lateral + depth_coupling * vertical
+    return COUPLING[level] * lateral + vertical
 
 
 def pair_sum(v, level):
@@ -82,6 +88,14 @@
     return out
 
 
+def messages(n, reach):
+    return [
+        (sign * far, min(n, reach - (far - 1) * n))
+        for far in range(1, -(-reach // n) + 1)
+        for sign in (-1, 1)
+    ]
+
+
 def kernel(plan, block, out, *scratch):
     nx_dev, nz_dev, comps, nz_own, nz, rows = (
         plan[k] for k in ("gx", "gz", "comps", "nz_own", "nz", "rows"))
@@ -96,7 +110,7 @@
         target = me + offset
         return jnp.logical_and(target >= 0, target < nx_dev)
 
-    offsets = (-1, 1, -2, 2)
+    offsets = [sign * far for far in range(1, plan["far"] + 1) for sign in (-1, 1)]
     barrier = pltpu.get_barrier_semaphore()
     expected = nz_dev - 1
     for step in range(1, nz_dev):
@@ -143,10 +157,11 @@
                 ref[row] = jnp.zeros(ref.shape[1:], ref.dtype)
         return run
 
-    def loop(low, high, body):
-        step = 2 if (high - low) % 2 == 0 else 1
+    def loop(low, high, body, step=None):
+        if step is None:
+            step = max(m for m in range(1, max(1, 30 // nz) + 1) if (high - low) % m == 0)
         count = (high - low) // step
-        if count <= 2 or step == 1:
+        if count <= 3:
             for index in range(count):
                 body(low + index * step, step)
         else:
@@ -193,7 +208,7 @@
             place = hc + (row - h) // 2
             coarse[place] = 0.25 * pair_sum(value[0] + value[1], level)
 
-        loop(h, h + rows[level], body)
+        loop(h, h + rows[level], body, 2)
 
     def restrict_density(level):
         fine, h = refs[f"s{level}"].at[dens], HALO[level]
@@ -201,26 +216,23 @@
         for index in range(rows[level + 1]):
             coarse[hc + index] = 0.25 * pair_sum(fine[h + 2 * index] + fine[h + 2 * index + 1], level)
 
-    def halo(level, ref, tag, c):
+    def halo(level, ref, tag, c, reach):
         p, h, n = 1 << level, HALO[level], rows[level]
         out_buf, in_buf = refs[f"out_{tag}"].at[c], refs[f"in_{tag}"].at[c]
         for row in range(n):
             for g, value in enumerate(pack([ref[h + row, z] for z in range(nz)], p)):
                 out_buf[row, g] = value
         finishes = []
-        width = min(n, 2)
-        for slot, offset in enumerate(offsets if n == 1 else offsets[:2]):
+        for slot, (offset, width) in enumerate(messages(n, reach)):
             first = 0 if offset < 0 else n - width
-            finishes.append((send(offset, out_buf.at[first:first + width], in_buf.at[slot]), slot, offset))
+            start = h - (offset - 1) * n - width if offset > 0 else h - offset * n
+            target = in_buf.at[slot, 0:width]
+            finishes.append((send(offset, out_buf.at[first:first + width], target), slot, start, width))
 
         def finish_all():
-            for finish, slot, offset in finishes:
-                if n == 1:
-                    start = h - offset
-                else:
-                    start = h + n if offset < 0 else h - width
-
-                def received(slot=slot, start=start):
+            for finish, slot, start, width in finishes:
+
+                def received(slot=slot, start=start, width=width):
                     for row in range(width):
                         groups = [in_buf[slot, row, g] for g in range(in_buf.shape[2])]
                         for z, value in enumerate(unpack(groups, nz, p)):
@@ -230,14 +242,13 @@
 
         return finish_all
 
-    def correct(level, c, field, dst):
+    def correct(level, c, field, dst, extra):
         h, n, hc = HALO[level], rows[level], HALO[level + 1]
-        coarse = refs[f"a{level + 1}"].at[c]
-        for index in range(rows[level + 1]):
+        coarse = refs[f"a{level + 1}"]
+        for index in range(-((extra + 1) // 2), (n + extra + 1) // 2):
             value = coarse[hc + index]
-            for part in range(2):
-                row = h + 2 * index + part
-                dst[row] = field[row] + value
+            for row in range(max(2 * index, -extra), min(2 * index + 2, n + extra)):
+                dst[h + row] = field[h + row] + value
 
     h0, n0 = HALO[0], rows[0]
     s0 = refs["s0"]
@@ -274,65 +285,67 @@
     density = {}
 
     def coarse_cycle(level, c, cycle):
-        s, a, b = (refs[f"{kind}{level}"].at[c] for kind in "sab")
-        h, n = HALO[level], rows[level]
-        finish = halo(level, s, f"s{level}_{cycle}", c)
+        s, a, b = refs[f"s{level}"].at[c], refs[f"a{level}"], refs[f"b{level}"].at[c]
+        n, reach, beyond = rows[level], REACH[cycle][level], BEYOND[cycle][level]
+        finish = halo(level, s, f"s{level}_{cycle}", c, reach)
         yield
         if cycle == 0 and c == 0:
             density.pop(level)()
-            weights(level, -2, n + 2)
+            weights(level, -reach, n + reach)
         finish()
-        first_sweep(level, c, a, 2)
-        sweep(level, c, a, b, 1)
+        first_sweep(level, c, a, reach)
+        sweep(level, c, a, b, reach - 1)
         if level == LEVELS - 1:
-            sweep(level, c, b, a, 0)
+            sweep(level, c, b, a, reach - 2)
             return
         restrict(level, c, b)
         yield from coarse_cycle(level + 1, c, cycle)
-        correct(level, c, b, a)
-        finish = halo(level, a, f"v{level}_{cycle}", c)
-        yield
-        finish()
-        sweep(level, c, a, b, 1)
-        sweep(level, c, b, a, 0)
+        correct(level, c, b, a, beyond + 2)
+        sweep(level, c, a, b, beyond + 1)
+        sweep(level, c, b, a, beyond)
 
     gathers = {c: gather(c) for c in [dens] + list(range(comps))}
 
     def component(c):
-        a0, b0 = refs["a0"].at[c], refs["b0"].at[c]
+        a0, b0 = refs["a0"], refs["b0"].at[c]
+        reach = REACH[0][0]
         if c == 0:
             gathers[dens]()
-            density["near"] = ends(s0.at[dens], 0, 2)
+            density["near"] = ends(s0.at[dens], 0, reach)
         gathers[c]()
-        finish = ends(s0.at[c], 0, 2)
+        finish = ends(s0.at[c], 0, reach)
         if c == 0:
             for level in range(LEVELS - 1):
                 restrict_density(level)
         yield
         if c == 0:
             density.pop("near")()
-            weights(0, -2, n0 + 2)
+            weights(0, -reach, n0 + reach)
             for level in range(1, LEVELS):
-                density[level] = halo(level, refs[f"s{level}"].at[dens], f"s{level}_0", dens)
-            density["far"] = ends(s0.at[dens], 2, 2)
+                density[level] = halo(level, refs[f"s{level}"].at[dens], f"s{level}_0", dens, REACH[0][level])
+            if not MERGED:
+                density["far"] = ends(s0.at[dens], 2, 2)
         finish()
-        far = ends(s0.at[c], 2, 2)
-        first_sweep(0, c, a0, 2)
-        sweep(0, c, a0, b0, 1)
+        if not MERGED:
+            far = ends(s0.at[c], 2, 2)
+        first_sweep(0, c, a0, reach)
+        sweep(0, c, a0, b0, reach - 1)
         for cycle in range(CYCLES):
             restrict(0, c, b0)
             yield from coarse_cycle(1, c, cycle)
             fresh = refs[f"f{cycle}"].at[c]
-            correct(0, c, b0, fresh)
-            finish = ends(fresh, 0, 5 if cycle < CYCLES - 1 else 2)
-            yield
-            if cycle == 0:
-                if c == 0:
-                    density.pop("far")()
-                    weights(0, -4, -2)
-                    weights(0, n0 + 2, n0 + 4)
-                far()
-            finish()
+            merged = MERGED and cycle == 0
+            correct(0, c, b0, fresh, 5 if merged else 0)
+            if not merged:
+                finish = ends(fresh, 0, 5 if cycle < CYCLES - 1 else 2)
+                yield
+                if cycle == 0:
+                    if c == 0:
+                        density.pop("far")()
+                        weights(0, -4, -2)
+                        weights(0, n0 + 2, n0 + 4)
+                    far()
+                finish()
             if cycle < CYCLES - 1:
                 sweep(0, c, fresh, a0, 4)
                 sweep(0, c, a0, b0, 3)
@@ -370,26 +383,25 @@
         total = rows[level] + 2 * HALO[level]
         buf(f"s{level}", comps + 1, total, nz)
         buf(f"w{level}", total, nz)
-        buf(f"a{level}", comps, total, nz)
+        buf(f"a{level}", total, nz)
         buf(f"b{level}", comps, total, nz)
     sems = (comps + 1) * (plan["gz"] - 1)
+    far = 1
     for cycle in range(CYCLES):
         buf(f"f{cycle}", comps, rows[0] + 2 * HALO[0], nz)
-        sems += comps * 2
         for level in range(1, LEVELS):
-            n = rows[level]
-            for kind, count in (("s", comps + (cycle == 0)), ("v", comps)):
-                if kind == "v" and level == LEVELS - 1:
-                    continue
-                groups = -(-nz // (1 << level))
-                buf(f"out_{kind}{level}_{cycle}", count, n, groups)
-                buf(f"in_{kind}{level}_{cycle}", count, 4 if n == 1 else 2, min(n, 2), groups)
-                sems += count * (4 if n == 1 else 2)
-    sems += (comps + 1) * 4
+            n, count = rows[level], comps + (cycle == 0)
+            groups = -(-nz // (1 << level))
+            sent = messages(n, REACH[cycle][level])
+            buf(f"out_s{level}_{cycle}", count, n, groups)
+            buf(f"in_s{level}_{cycle}", count, len(sent), sent[0][1], groups)
+            sems += count * len(sent)
+            far = max(far, sent[-1][0])
+    sems += (comps + 1) * 2 + (comps * 2 if MERGED else (comps + 1) * 2 + comps * 4)
     shapes["send"] = pltpu.SemaphoreType.DMA((sems,))
     shapes["recv"] = pltpu.SemaphoreType.DMA((sems,))
     shapes["local"] = pltpu.SemaphoreType.DMA((comps + 1,))
-    plan = dict(plan, comps=comps, nz_own=nz_own, nz=nz, rows=rows, names=list(shapes))
+    plan = dict(plan, far=far, comps=comps, nz_own=nz_own, nz=nz, rows=rows, names=list(shapes))
     result = pl.pallas_call(
         functools.partial(kernel, plan),
         out_shape=jax.ShapeDtypeStruct((comps, n0, nz_own, SUB, LANE), jnp.float32),

time: 80.6 us -> 77.6 us (0.963)
  Pallas kernels: 75.9 us -> 72.3 us
    pallas_call x1, Pallas kernels: 75.9 us -> 72.3 us  [shards(): pl.pallas_call(functools.partial(kernel, plan), out_shape=jax.ShapeDtypeS...]
where the time goes in v2:
time: 77.6 us; the launch traced here: 76.7 us
  Pallas kernels  72.3 us (93%)
  local copies, waits for them, and re-layouts  3.68 us (5%)
    pallas_call x1, Pallas kernels, shards(): pl.pallas_call(functools.partial(kernel, plan), out_shape=jax.ShapeDtypeS...  72.3 us
    unnamed x2, local copies, waits for them, and re-layouts  1.93 us

profile of v2, /device:TPU:3, one launch (start us, length us, event | category | flops | bytes accessed | tf_op | source)
XLA Modules:
  0.0 76.7 jit_solution(11316229266587005131)
XLA Ops:
  0.0 0.9 %copy.14 = f32[3,8,8,128]{3,2,1,0:T(8,128)S(1)} copy(f32[3,8,8,128]{3,1,2,0:T(8,128)} %bitcast.20) | data formatting | bytes 196608
  0.9 1.0 %copy.10 = f32[9,8,8,128]{3,2,1,0:T(8,128)S(1)} copy(f32[9,8,8,128]{3,1,2,0:T(8,128)} %bitcast.19) | data formatting | bytes 589824
  1.9 0.8 copy_bitcast_fusion.block
  2.7 72.3 %shard_map.28 = f32[3,8,3,8,128]{4,3,2,1,0:T(8,128)} custom-call(f32[4,8,3,8,128]{4,3,2,1,0:T(8,128)} %copy_bitcast_fusion.block), custom_call_target="tpu_custom_call" | custom-call | tf_op jit(solution)/shard_map/pallas_call | solution.py:405
  75.0 1.0 %copy.8 = f32[3,3,8,8,128]{4,3,2,1,0:T(8,128)S(1)} copy(f32[3,3,8,8,128]{4,3,1,2,0:T(8,128)} %bitcast.17) | data formatting | bytes 589824 | tf_op jit(solution)/shard_map/transpose | solution.py:414
  75.9 0.8 reshape.7

commit v3 on v2

--- a/solution.py
+++ b/solution.py
@@ -43,10 +43,29 @@
     return total.reshape(shape)
 
 
-def neighbours(strip, level):
+def turn_classes(v, level, classes, step):
+    if level == 0:
+        return v
+    shape = v.shape
+    v = v.reshape((-1, SUB, LANE))
+    _, lane = iotas()
+    place = lane & ((1 << level) - 1)
+    if step > 0:
+        v = jnp.where(place < classes - 1, pltpu.roll(v, LANE - 1, 2), pltpu.roll(v, classes - 1, 2))
+    else:
+        v = jnp.where(place > 0, pltpu.roll(v, 1, 2), pltpu.roll(v, LANE - (classes - 1), 2))
+    return v.reshape(shape)
+
+
+def neighbours(strip, level, classes):
     v = strip[1:-1]
     lateral = strip[:-2] + strip[2:] + y_sum(v, 1 << level)
-    vertical = jnp.concatenate([v[:, -1:], v[:, :-1]], 1) + jnp.concatenate([v[:, 1:], v[:, :1]], 1)
+    before = turn_classes(v[:, -1:], level, classes, -1)
+    after = turn_classes(v[:, :1], level, classes, 1)
+    if v.shape[1] > 1:
+        before = jnp.concatenate([before, v[:, :-1]], 1)
+        after = jnp.concatenate([v[:, 1:], after], 1)
+    vertical = before + after
     return COUPLING[level] * lateral + vertical
 
 
@@ -105,6 +124,12 @@
     z0 = mz * nz_own
     counter = [0]
     dens = comps
+    groups = plan["groups"]
+    classes = [nz // g for g in groups]
+
+    def repack(value, level, target):
+        planes = unpack([value[g] for g in range(value.shape[0])], nz, 1 << level)
+        return jnp.stack(pack(planes, 1 << target))
 
     def there(offset):
         target = me + offset
@@ -157,9 +182,9 @@
                 ref[row] = jnp.zeros(ref.shape[1:], ref.dtype)
         return run
 
-    def loop(low, high, body, step=None):
+    def loop(low, high, body, step=None, width=nz):
         if step is None:
-            step = max(m for m in range(1, max(1, 30 // nz) + 1) if (high - low) % m == 0)
+            step = max(m for m in range(1, max(1, 30 // width) + 1) if (high - low) % m == 0)
         count = (high - low) // step
         if count <= 3:
             for index in range(count):
@@ -182,7 +207,7 @@
             here = pl.ds(row, m)
             dst[here] = w[here] * s[here]
 
-        loop(h - extra, h + n + extra, body)
+        loop(h - extra, h + n + extra, body, None, groups[level])
 
     def sweep(level, c, src, dst, extra, last=False):
         s, w, h, n = refs[f"s{level}"].at[c], refs[f"w{level}"], HALO[level], rows[level]
@@ -190,11 +215,11 @@
         def body(row, m):
             here = pl.ds(row, m)
             strip = src[pl.ds(row - 1, m + 2)]
-            dst[here] = (1.0 - relaxation) * strip[1:-1] + w[here] * (s[here] + neighbours(strip, level))
+            dst[here] = (1.0 - relaxation) * strip[1:-1] + w[here] * (s[here] + neighbours(strip, level, classes[level]))
             if last:
                 out[c, pl.ds(row - h, m)] = dst[here, pl.ds(z0, nz_own)]
 
-        loop(h - extra, h + n + extra, body)
+        loop(h - extra, h + n + extra, body, None, groups[level])
 
     def restrict(level, c, src):
         s, d, h = refs[f"s{level}"].at[c], refs[f"s{level}"].at[dens], HALO[level]
@@ -204,9 +229,9 @@
             here = pl.ds(row, m)
             strip = src[pl.ds(row - 1, m + 2)]
             diagonal = d[here] + 4.0 * COUPLING[level] + 2.0 * depth_coupling
-            value = s[here] - diagonal * strip[1:-1] + neighbours(strip, level)
+            value = s[here] - diagonal * strip[1:-1] + neighbours(strip, level, classes[level])
             place = hc + (row - h) // 2
-            coarse[place] = 0.25 * pair_sum(value[0] + value[1], level)
+            coarse[place] = repack(0.25 * pair_sum(value[0] + value[1], level), level, level + 1)
 
         loop(h, h + rows[level], body, 2)
 
@@ -214,29 +239,25 @@
         fine, h = refs[f"s{level}"].at[dens], HALO[level]
         coarse, hc = refs[f"s{level + 1}"].at[dens], HALO[level + 1]
         for index in range(rows[level + 1]):
-            coarse[hc + index] = 0.25 * pair_sum(fine[h + 2 * index] + fine[h + 2 * index + 1], level)
+            total = fine[h + 2 * index] + fine[h + 2 * index + 1]
+            coarse[hc + index] = repack(0.25 * pair_sum(total, level), level, level + 1)
 
     def halo(level, ref, tag, c, reach):
-        p, h, n = 1 << level, HALO[level], rows[level]
-        out_buf, in_buf = refs[f"out_{tag}"].at[c], refs[f"in_{tag}"].at[c]
-        for row in range(n):
-            for g, value in enumerate(pack([ref[h + row, z] for z in range(nz)], p)):
-                out_buf[row, g] = value
+        h, n = HALO[level], rows[level]
+        in_buf = refs[f"in_{tag}"].at[c]
         finishes = []
         for slot, (offset, width) in enumerate(messages(n, reach)):
-            first = 0 if offset < 0 else n - width
+            first = h if offset < 0 else h + n - width
             start = h - (offset - 1) * n - width if offset > 0 else h - offset * n
             target = in_buf.at[slot, 0:width]
-            finishes.append((send(offset, out_buf.at[first:first + width], target), slot, start, width))
+            finishes.append((send(offset, ref.at[first:first + width], target), slot, start, width))
 
         def finish_all():
             for finish, slot, start, width in finishes:
 
                 def received(slot=slot, start=start, width=width):
                     for row in range(width):
-                        groups = [in_buf[slot, row, g] for g in range(in_buf.shape[2])]
-                        for z, value in enumerate(unpack(groups, nz, p)):
-                            ref[start + row, z] = value
+                        ref[start + row] = in_buf[slot, row]
 
                 finish(received, zero_rows(ref, start, start + width))
 
@@ -246,7 +267,7 @@
         h, n, hc = HALO[level], rows[level], HALO[level + 1]
         coarse = refs[f"a{level + 1}"]
         for index in range(-((extra + 1) // 2), (n + extra + 1) // 2):
-            value = coarse[hc + index]
+            value = repack(coarse[hc + index], level + 1, level)
             for row in range(max(2 * index, -extra), min(2 * index + 2, n + extra)):
                 dst[h + row] = field[h + row] + value
 
@@ -374,6 +395,8 @@
     block = block.reshape(comps + 1, nz_own, n0, SUB, LANE).transpose(0, 2, 1, 3, 4)
     nz = nz_own * plan["gz"]
     rows = [n0 >> level for level in range(LEVELS)]
+    groups = [-(-nz // (1 << level)) for level in range(LEVELS)]
+    assert all(nz % g == 0 for g in groups)
     shapes = {}
 
     def buf(name, *shape):
@@ -381,27 +404,25 @@
 
     for level in range(LEVELS):
         total = rows[level] + 2 * HALO[level]
-        buf(f"s{level}", comps + 1, total, nz)
-        buf(f"w{level}", total, nz)
-        buf(f"a{level}", total, nz)
-        buf(f"b{level}", comps, total, nz)
+        buf(f"s{level}", comps + 1, total, groups[level])
+        buf(f"w{level}", total, groups[level])
+        buf(f"a{level}", total, groups[level])
+        buf(f"b{level}", comps, total, groups[level])
     sems = (comps + 1) * (plan["gz"] - 1)
     far = 1
     for cycle in range(CYCLES):
         buf(f"f{cycle}", comps, rows[0] + 2 * HALO[0], nz)
         for level in range(1, LEVELS):
             n, count = rows[level], comps + (cycle == 0)
-            groups = -(-nz // (1 << level))
             sent = messages(n, REACH[cycle][level])
-            buf(f"out_s{level}_{cycle}", count, n, groups)
-            buf(f"in_s{level}_{cycle}", count, len(sent), sent[0][1], groups)
+            buf(f"in_s{level}_{cycle}", count, len(sent), sent[0][1], groups[level])
             sems += count * len(sent)
             far = max(far, sent[-1][0])
     sems += (comps + 1) * 2 + (comps * 2 if MERGED else (comps + 1) * 2 + comps * 4)
     shapes["send"] = pltpu.SemaphoreType.DMA((sems,))
     shapes["recv"] = pltpu.SemaphoreType.DMA((sems,))
     shapes["local"] = pltpu.SemaphoreType.DMA((comps + 1,))
-    plan = dict(plan, far=far, comps=comps, nz_own=nz_own, nz=nz, rows=rows, names=list(shapes))
+    plan = dict(plan, far=far, groups=groups, comps=comps, nz_own=nz_own, nz=nz, rows=rows, names=list(shapes))
     result = pl.pallas_call(
         functools.partial(kernel, plan),
         out_shape=jax.ShapeDtypeStruct((comps, n0, nz_own, SUB, LANE), jnp.float32),

time: 77.6 us -> 70.1 us (0.903)
  Pallas kernels: 72.3 us -> 64.8 us
    pallas_call x1, Pallas kernels: 72.3 us -> 64.8 us  [shards(): pl.pallas_call(functools.partial(kernel, plan), out_shape=jax.ShapeDtypeS...]
where the time goes in v3:
time: 70.1 us; the launch traced here: 69.3 us
  Pallas kernels  64.8 us (92%)
  local copies, waits for them, and re-layouts  3.68 us (5%)
  other arithmetic  0.77 us (1%)
    pallas_call x1, Pallas kernels, shards(): pl.pallas_call(functools.partial(kernel, plan), out_shape=jax.ShapeDtypeS...  64.8 us
    unnamed x2, local copies, waits for them, and re-layouts  1.93 us

profile of v3, /device:TPU:3, one launch (start us, length us, event | category | flops | bytes accessed | tf_op | source)
XLA Modules:
  0.0 69.3 jit_solution(11153541735582464876)
XLA Ops:
  0.0 0.9 %copy.14 = f32[3,8,8,128]{3,2,1,0:T(8,128)S(1)} copy(f32[3,8,8,128]{3,1,2,0:T(8,128)} %bitcast.20) | data formatting | bytes 196608
  0.9 1.0 %copy.10 = f32[9,8,8,128]{3,2,1,0:T(8,128)S(1)} copy(f32[9,8,8,128]{3,1,2,0:T(8,128)} %bitcast.19) | data formatting | bytes 589824
  1.9 0.8 %copy_bitcast_fusion.block = f32[4,8,3,8,128]{4,3,2,1,0:T(8,128)} fusion(f32[1,3,8,8,128]{4,3,2,1,0:T(8,128)S(1)} %bitcast.18, f32[3,3,8,8,128]{4,3,2,1,0:T(8,128)S(1)} %bitcast.16), kind=kLoop, calls=%fused_computation.1 | loop fusion | flops 98304 | bytes 786432 | tf_op jit(solution)/shard_map/transpose | solution.py:395
  2.7 64.8 %shard_map.28 = f32[3,8,3,8,128]{4,3,2,1,0:T(8,128)} custom-call(f32[4,8,3,8,128]{4,3,2,1,0:T(8,128)} %copy_bitcast_fusion.block), custom_call_target="tpu_custom_call" | custom-call | tf_op jit(solution)/shard_map/pallas_call | solution.py:426
  67.5 1.0 %copy.8 = f32[3,3,8,8,128]{4,3,2,1,0:T(8,128)S(1)} copy(f32[3,3,8,8,128]{4,3,1,2,0:T(8,128)} %bitcast.17) | data formatting | bytes 589824 | tf_op jit(solution)/shard_map/transpose | solution.py:435
  68.5 0.8 %reshape.7 = f32[3,3,8,1024]{3,2,1,0:T(8,128)} reshape(f32[3,3,8,8,128]{4,3,2,1,0:T(8,128)S(1)} %copy.8) | data formatting | bytes 589824 | tf_op jit(solution)/shard_map/reshape | solution.py:435
